TPU v7x, 32 devices: a whole 2x2x4 slice. The times are simulated.
32 devices in a mesh: groups: 2 (over x), dp: 8 (over z, y), tensor: 2 (over core).
Axes of the slice: x: 2, y: 2, z: 4, core: 2. Of those that a mesh axis runs over, the one named last changes fastest.
Arguments:
- hidden_states: bfloat16 [3584, 5120], P(('groups', 'dp'), 'tensor'), parts along dimension 0, may hold values from -6 to 6
- input_gain: float32 [5120], replicated, may hold values from 0.1 to 1.9
- q_weight: bfloat16 [5120, 512], P(None, 'tensor'), may hold values from -0.078125 to 0.078125
- k_weight: bfloat16 [5120, 256], P(None, 'tensor'), may hold values from -0.078125 to 0.078125
- v_weight: bfloat16 [5120, 256], P(None, 'tensor'), may hold values from -0.078125 to 0.078125
- o_weight: bfloat16 [512, 5120], P('tensor'), may hold values from -0.25 to 0.25
- q_gain: float32 [128], replicated, may hold values from 0.6 to 13
- k_gain: float32 [128], replicated, may hold values from 0.6 to 13
- seq_lens: int32 [16, 5], P('groups'), parts along dimension 0, may hold values from 1 to 160, as said below
- dest: int32 [16, 5], P('groups'), parts along dimension 0, may hold values from 0 to 7, as said below
Outputs:
- mixed: bfloat16 [2560, 5120], P(('groups', 'dp'), 'tensor'), parts along dimension 0
There are 2 independent parts, one for each index of `groups`. A program takes and returns all parts, laid end to end along the dimension named above; an argument that names none is the same for every part. Nothing has to cross between parts.
Inputs may be any that keep to these rules, and one draw needn't show every extreme that they name: `seq_lens`: each replica's sequences lie packed from row 0 of its block in slot order. `dest`: slot 0 never moves. A replica either sends sequences or receives them, never both. At most 16 tokens in all go from one replica to any one other, and at most 160 tokens are processed by one replica; both bounds are reached.
All inputs are finite; a program needn't handle non-finite values.
Results may differ from a plain program's by a relative error of at most 0.004.
The roundings to bfloat16 on the way count: a program that leaves them out, or rounds other values in their place, can miss the bound.
Values may be sent and summed in bfloat16 or wider, within the bound.
A program may use at most 128 MiB of HBM per device.

v0:
```python
import jax
import jax.numpy as jnp
from jax import lax
from jax.sharding import PartitionSpec as P

HD = 128
CAPP = 16
LONG = 160
SHORT = 8
EPSILON = 1e-06
ROPE_BASE = 1000000.0
MASKED_SCORE = -1e30


def rms_scale(entries, gain):
    mean_square = jnp.mean(entries * entries, axis=-1, keepdims=True)
    return entries * lax.rsqrt(mean_square + EPSILON) * gain


def rotation(positions, width):
    half_head = width // 2
    frequency = ROPE_BASE ** (-2.0 * jnp.arange(half_head, dtype=jnp.float32) / width)
    angles = positions.astype(jnp.float32)[:, None] * frequency[None, :]
    return (jnp.cos(angles), jnp.sin(angles))


def rotate(entries, cosine, sine_part):
    half_head = entries.shape[-1] // 2
    first_half = entries[..., :half_head]
    second_half = entries[..., half_head:]
    return jnp.concatenate(
        [
            first_half * cosine - second_half * sine_part,
            second_half * cosine + first_half * sine_part,
        ],
        axis=-1,
    )


def sequence_table(seq_lens, dest):
    replicas, slots = seq_lens.shape
    lengths = seq_lens.reshape(-1)
    offsets = (jnp.cumsum(seq_lens, axis=1) - seq_lens).reshape(-1)
    source = jnp.broadcast_to(
        jnp.arange(replicas, dtype=jnp.int32)[:, None], (replicas, slots)
    ).reshape(-1)
    slot_index = jnp.broadcast_to(
        jnp.arange(slots, dtype=jnp.int32)[None, :], (replicas, slots)
    ).reshape(-1)
    target = dest.reshape(-1)
    order_key = (source - target) % replicas * slots + slot_index
    earlier = (target[None, :] == target[:, None]) & (order_key[None, :] < order_key[:, None])
    begins = jnp.sum(jnp.where(earlier, lengths[None, :], 0), axis=1)
    return (source, slot_index, lengths, target, offsets, begins)


def widen(half_rows):
    return lax.all_gather(half_rows, "tensor", axis=1, tiled=True)


def project(full_rows, positions, input_gain, q_weight, k_weight, v_weight, q_gain, k_gain):
    row_count = full_rows.shape[0]
    normed = rms_scale(full_rows.astype(jnp.float32), input_gain).astype(jnp.bfloat16)
    cosine, sine_part = rotation(positions, HD)
    queries = jnp.dot(normed, q_weight, preferred_element_type=jnp.float32).reshape(
        row_count, -1, HD
    )
    queries = rotate(rms_scale(queries, q_gain), cosine[:, None, :], sine_part[:, None, :]).astype(
        jnp.bfloat16
    )
    key_rows = jnp.dot(normed, k_weight, preferred_element_type=jnp.float32)
    key_rows = rotate(rms_scale(key_rows, k_gain), cosine, sine_part).astype(jnp.bfloat16)
    value_rows = jnp.dot(normed, v_weight, preferred_element_type=jnp.float32).astype(jnp.bfloat16)
    return (queries, key_rows, value_rows)


def attend(queries, key_rows, value_rows, segment, position):
    scores = jnp.einsum(
        "qhd,kd->hqk", queries, key_rows, preferred_element_type=jnp.float32
    ) * queries.shape[-1] ** (-0.5)
    allowed = (segment[:, None] == segment[None, :]) & (position[None, :] <= position[:, None])
    scores = jnp.where(allowed[None], scores, MASKED_SCORE)
    row_max = jnp.max(scores, axis=2, keepdims=True)
    exp_scores = jnp.exp(scores - row_max)
    weights = (exp_scores / jnp.sum(exp_scores, axis=2, keepdims=True)).astype(jnp.bfloat16)
    return jnp.einsum("hqk,kd->qhd", weights, value_rows, preferred_element_type=jnp.float32)


def per_device(
    hidden_states,
    input_gain,
    q_weight,
    k_weight,
    v_weight,
    o_weight,
    q_gain,
    k_gain,
    seq_lens,
    dest,
):
    replicas = lax.axis_size("dp")
    replica = lax.axis_index("dp")
    tensor_part = lax.axis_index("tensor")
    home_rows, half_width = hidden_states.shape
    slots = seq_lens.shape[1]
    work_rows = max(LONG, slots * SHORT + (slots - 1) * CAPP)
    source, slot_index, lengths, target, offsets, begins = sequence_table(seq_lens, dest)
    seq_ident = jnp.arange(lengths.shape[0], dtype=jnp.int32)
    shipped_seq = source != target
    pair_earlier = (
        (source[None, :] == source[:, None])
        & (target[None, :] == target[:, None])
        & (slot_index[None, :] < slot_index[:, None])
    )
    send_begin = jnp.sum(jnp.where(pair_earlier, lengths[None, :], 0), axis=1)
    peer_ids = jnp.arange(replicas, dtype=jnp.int32)[:, None, None]
    slot_rows = jnp.arange(CAPP, dtype=jnp.int32)[None, :, None]
    inside = (send_begin <= slot_rows) & (slot_rows < send_begin + lengths)
    outgoing = inside & shipped_seq & (source == replica) & (target == peer_ids)
    send_rows = jnp.sum(jnp.where(outgoing, offsets + slot_rows - send_begin, 0), axis=2).reshape(
        -1
    )
    incoming = inside & shipped_seq & (target == replica) & (source == peer_ids)
    arrive_live = jnp.any(incoming, axis=2)
    arrive_seg = jnp.where(arrive_live, jnp.sum(jnp.where(incoming, seq_ident, 0), axis=2), -1)
    arrive_pos = jnp.sum(jnp.where(incoming, slot_rows - send_begin, 0), axis=2)
    home_ids = jnp.arange(home_rows, dtype=jnp.int32)[:, None]
    resident = (source == replica) & (offsets <= home_ids) & (home_ids < offsets + lengths)
    home_live = jnp.any(resident, axis=1)
    home_seg = jnp.where(home_live, jnp.sum(jnp.where(resident, seq_ident, 0), axis=1), -1)
    home_pos = jnp.sum(jnp.where(resident, home_ids - offsets, 0), axis=1)
    work_ids = jnp.arange(work_rows, dtype=jnp.int32)[:, None]
    placed = (target == replica) & (begins <= work_ids) & (work_ids < begins + lengths)
    work_live = jnp.any(placed, axis=1)
    work_pos = jnp.sum(jnp.where(placed, work_ids - begins, 0), axis=1)
    pool_base = jnp.where(source == replica, offsets, home_rows + source * CAPP + send_begin)
    pool_row = jnp.sum(jnp.where(placed, pool_base, 0), axis=1) + work_pos
    home_full = widen(hidden_states)
    outbound = jnp.take(home_full, send_rows, axis=0).reshape(replicas, CAPP, -1)
    arrived = lax.all_to_all(outbound, "dp", split_axis=0, concat_axis=0, tiled=True)
    pool_full = jnp.concatenate([home_full, arrived.reshape(replicas * CAPP, -1)], axis=0)
    pool_half = lax.dynamic_slice_in_dim(pool_full, tensor_part * half_width, half_width, 1)
    pool_pos = jnp.concatenate([home_pos, arrive_pos.reshape(-1)], axis=0)
    queries, key_rows, value_rows = project(
        pool_full, pool_pos, input_gain, q_weight, k_weight, v_weight, q_gain, k_gain
    )
    home_out = attend(
        queries[:home_rows], key_rows[:home_rows], value_rows[:home_rows], home_seg, home_pos
    )
    arrive_out = jax.vmap(attend)(
        queries[home_rows:].reshape(replicas, CAPP, -1, HD),
        key_rows[home_rows:].reshape(replicas, CAPP, HD),
        value_rows[home_rows:].reshape(replicas, CAPP, HD),
        arrive_seg,
        arrive_pos,
    )
    head_out = jnp.concatenate([home_out, arrive_out.reshape(replicas * CAPP, -1, HD)], axis=0)
    head_out = head_out.reshape(home_rows + replicas * CAPP, -1).astype(jnp.bfloat16)
    all_heads = lax.all_gather(head_out, "tensor", axis=1, tiled=True)
    own_columns = lax.all_to_all(o_weight, "tensor", split_axis=1, concat_axis=0, tiled=True)
    summed = jnp.dot(all_heads, own_columns, preferred_element_type=jnp.float32)
    mixed_pool = pool_half.astype(jnp.float32) + summed
    mixed = jnp.where(work_live[:, None], jnp.take(mixed_pool, pool_row, axis=0), 0.0)
    return mixed.astype(jnp.bfloat16)


def solution(mesh):
    return jax.shard_map(
        per_device,
        mesh=mesh,
        in_specs=(
            P(("groups", "dp"), "tensor"),
            P(),
            P(None, "tensor"),
            P(None, "tensor"),
            P(None, "tensor"),
            P("tensor", None),
            P(),
            P(),
            P("groups", None),
            P("groups", None),
        ),
        out_specs=P(("groups", "dp"), "tensor"),
        check_vma=False,
    )
```

profile of v0, /device:TPU:0, one launch (start us, length us, event | category | flops | bytes accessed | tf_op | source)
XLA Modules:
  0.0 107.7 jit_solution(4255287312289752939)
XLA Ops:
  6.5 0.0 copy-start
  6.5 0.0 all-gather.2.cloned.1.call-start
  6.5 0.7 all-gather.2.cloned.1.call-update
  7.3 4.5 %copy.54 = bf16[256,5120]{0,1:T(8,128)(2,1)} copy(bf16[256,5120]{1,0:T(8,128)(2,1)} %param.15) | data formatting | bytes 5242880 | tf_op args[5]
  11.7 5.1 %all-to-all-start.1 = ((bf16[256,2,2560]{0,2,1:T(8,128)(2,1)}), bf16[256,2,2560]{0,2,1:T(8,128)(2,1)}, u32[]{:S(2)}, u32[]{:S(2)}) async-start(bf16[256,2,2560]{0,2,1:T(8,128)(2,1)} %bitcast.82), calls=%async_computation.1 | async-start | bytes 5242880 | tf_op jit(solution)/shard_map/all_to_all | solution.py:160
  16.9 0.1 reshape.679
  17.0 0.0 copy-done.6
  17.0 0.1 reshape.678
  17.0 0.1 reshape.680
  17.1 0.0 copy-done.4
  17.1 0.1 broadcast_in_dim.197
  17.2 0.2 reduce_window_sum.11
  17.4 0.1 reshape.681
  17.5 0.2 select_reduce_fusion.6
  17.7 0.2 select_reduce_fusion
  18.0 0.1 reshape.682
  18.1 4.4 %all-gather.2.cloned.1.call-done = bf16[224,5120]{1,0:T(8,128)(2,1)} async-done(((bf16[224,2560]{1,0:T(8,128)(2,1)}), bf16[224,5120]{1,0:T(8,128)(2,1)}) %all-gather.2.cloned.1.call-update) | async-done | bytes 2293776 | tf_op jit(solution)/shard_map/all_gather | solution.py:58
  22.5 5.6 %gather_fusion = bf16[128,5120]{1,0:T(8,128)(2,1)} fusion(bf16[224,5120]{1,0:T(8,128)(2,1)} %all-gather.2.cloned.1.call-done, s32[1024]{0:T(1024)S(1)} %pad_clamp_fusion.1), kind=kCustom, calls=%fused_computation | custom fusion | bytes 2621952 | tf_op jit(solution)/shard_map/jit(_take)/gather | solution.py:139
  28.1 2.6 %broadcast_select_fusion = bf16[8,16,5120]{2,1,0:T(8,128)(2,1)} fusion(bf16[8,16,5120]{2,1,0:T(8,128)(2,1)} %bitcast.83, pred[8,16]{1,0:T(8,128)(4,1)S(1)} %compare_and_fusion.4), kind=kLoop, calls=%fused_computation.15 | loop fusion | flops 655360 | bytes 2621568 | tf_op jit(solution)/shard_map/jit(_take)/select_n | solution.py:139
  30.7 0.0 all-to-all-done.1
  30.7 6.5 %all-to-all-start = ((bf16[8,16,5120]{2,1,0:T(8,128)(2,1)}), bf16[8,16,5120]{2,1,0:T(8,128)(2,1)}, u32[]{:S(2)}, u32[]{:S(2)}) async-start(bf16[8,16,5120]{2,1,0:T(8,128)(2,1)} %broadcast_select_fusion), calls=%async_computation | async-start | bytes 2621440 | tf_op jit(solution)/shard_map/all_to_all | solution.py:140
  37.2 0.3 fusion.20
  37.6 0.1 concatenate.30
  37.6 4.4 %copy.55 = bf16[2,256,2560]{2,1,0:T(8,128)(2,1)} copy(bf16[2,256,2560]{1,2,0:T(8,128)(2,1)} %bitcast.17) | data formatting | bytes 5242880 | tf_op jit(solution)/shard_map/all_to_all | solution.py:160
  42.0 0.5 multiply_power_fusion
  42.6 0.1 select_reduce_fusion.2
  42.7 0.1 add_convert_fusion.2
  42.8 0.1 select_reduce_fusion.3
  42.9 0.2 and_reduce_fusion
  43.1 0.1 fusion.59
  43.2 0.1 fusion.58
  43.4 0.1 compare_and_fusion.1
  43.5 0.8 compare_and_fusion
  44.2 24.8 %all-to-all-done = bf16[8,16,5120]{2,1,0:T(8,128)(2,1)} async-done(((bf16[8,16,5120]{2,1,0:T(8,128)(2,1)}), bf16[8,16,5120]{2,1,0:T(8,128)(2,1)}, u32[]{:S(2)}, u32[]{:S(2)}) %all-to-all-start) | async-done | bytes 1310752 | tf_op jit(solution)/shard_map/all_to_all | solution.py:140
  69.1 3.0 %fusion.2 = f32[352]{0:T(512)S(1)} fusion(bf16[128,5120]{1,0:T(8,128)(2,1)} %bitcast.2, bf16[224,5120]{1,0:T(8,128)(2,1)} %all-gather.2.cloned.1.call-done), kind=kLoop, calls=%fused_computation.6 | loop fusion | flops 10813088 | bytes 3605888 | tf_op jit(solution)/shard_map/reduce_sum | solution.py:16
  72.1 2.1 %fusion.4 = bf16[352,5120]{1,0:T(8,128)(2,1)S(1)} fusion(f32[5120]{0:T(1024)S(1)} %copy-done.5, f32[352]{0:T(512)S(1)} %add_rsqrt_fusion.2, bf16[128,5120]{1,0:T(8,128)(2,1)} %bitcast.2, bf16[224,5120]{1,0:T(8,128)(2,1)S(1)} %copy-done.1), kind=kLoop, calls=%fused_computation.8 | loop fusion | flops 12615680 | bytes 7230848 | tf_op jit(solution)/shard_map/convert_element_type | solution.py:63
  74.2 0.0 copy-start.2
  74.2 1.8 %copy-done.2 = bf16[352,5120]{1,0:T(8,128)(2,1)} copy-done((bf16[352,5120]{1,0:T(8,128)(2,1)}, bf16[352,5120]{1,0:T(8,128)(2,1)S(1)}, u32[]{:S(2)}) %copy-start.2) | copy-done | bytes 3604504
  76.0 1.1 %fusion.68 = f32[352,256]{1,0:T(8,128)S(1)} fusion(bf16[352,5120]{1,0:T(8,128)(2,1)S(1)} %fusion.4, bf16[5120,256]{1,0:T(8,128)(2,1)S(1)} %copy-done), kind=kOutput, calls=%fused_computation.131 | convolution fusion | flops 922746880 | bytes 6586368 | tf_op jit(solution)/shard_map/dot_general | solution.py:65
  77.2 0.2 reshape.684
  77.4 0.4 multiply_reduce_fusion
  77.8 0.1 copy.47
  77.9 0.0 copy-start.7
  77.9 0.0 copy-start.8
  77.9 3.6 %multiply_reduce_fusion.1 = (f32[352]{0:T(512)S(1)}, f32[352,128]{1,0:T(8,128)S(1)}) fusion(bf16[352,5120]{1,0:T(8,128)(2,1)} %copy-done.2, bf16[5120,128]{1,0:T(8,128)(2,1)} %param.13), kind=kOutput, calls=%fused_computation.46 | convolution fusion | flops 461463200 | bytes 5096832 | tf_op jit(solution)/shard_map/dot_general | solution.py:71
  81.6 0.2 fusion.16
  81.8 0.1 multiply_multiply_fusion
  81.9 0.0 copy-done.9
  81.9 0.8 multiply_cosine_fusion
  82.7 0.2 subtract_convert_fusion
  82.9 0.1 pad_maximum_fusion.2
  83.0 0.1 pad_maximum_fusion.3
  83.0 0.3 fusion.13
  83.3 0.3 fusion.60
  83.6 0.0 copy-done.3
  83.6 1.2 %fusion.63 = (f32[2,224]{1,0:T(2,128)S(1)}, f32[2,224,224]{1,2,0:T(8,128)}) fusion(pred[224,224]{0,1:T(8,128)(4,1)S(1)} %copy-done.3, bf16[352,2,64]{2,0,1:T(8,128)(2,1)S(1)} %get-tuple-element.15, bf16[352,2,64]{2,0,1:T(8,128)(2,1)S(1)} %get-tuple-element.16, bf16[352,64]{1,0:T(8,128)(2,1)S(1)} %get-tuple-element.22, ...), kind=kOutput, calls=%fused_computation.130 | convolution fusion | flops 26435808 | bytes 723712 | tf_op jit(solution)/shard_map/sub | solution.py:84
  84.8 3.5 %convolution_convert_fusion.1 = bf16[352,128]{1,0:T(8,128)(2,1)S(1)} fusion(bf16[352,5120]{1,0:T(8,128)(2,1)} %copy-done.2, bf16[5120,128]{1,0:T(8,128)(2,1)} %param.14), kind=kOutput, calls=%fused_computation.23 | convolution fusion | flops 461418496 | bytes 5005312 | tf_op jit(solution)/shard_map/dot_general | solution.py:73
  88.4 0.3 fusion.14
  88.7 0.2 fusion.15
  88.9 0.1 copy.53
  89.0 2.2 %all_gather.7 = bf16[352,512]{1,0:T(8,128)(2,1)S(1)} all-gather(bf16[352,256]{1,0:T(8,128)(2,1)S(1)} %pad_maximum_fusion.1), channel_id=1, replica_groups=mesh['groups'=2,'dp'=8,'tensor'=2] {'tensor'}, dimensions={1}, use_global_device_ids=true | all-gather | bytes 540672 | tf_op jit(solution)/shard_map/all_gather | solution.py:159
  91.3 4.5 %convolution_add_fusion = bf16[352,2560]{1,0:T(8,128)(2,1)} fusion(bf16[352,512]{1,0:T(8,128)(2,1)S(1)} %all_gather.7, bf16[512,2560]{1,0:T(8,128)(2,1)} %bitcast.84, s32[]{:T(128)S(6)} %select_n.145, bf16[224,5120]{1,0:T(8,128)(2,1)} %all-gather.2.cloned.1.call-done, bf16[128,5120]{1,0:T(8,128)(2,1)} %bitcast.2), kind=kOutput, calls=%fused_computation.9 | convolution fusion | flops 928153600 | bytes 8388612 | tf_op jit(solution)/shard_map/dot_general | solution.py:161
  95.8 3.6 %gather_fusion.1 = bf16[160,2560]{1,0:T(8,128)(2,1)S(1)} fusion(bf16[352,2560]{1,0:T(8,128)(2,1)} %convolution_add_fusion, s32[1024]{0:T(1024)S(1)} %pad_clamp_fusion), kind=kCustom, calls=%fused_computation.1 | custom fusion | bytes 1639040 | tf_op jit(solution)/shard_map/jit(_take)/gather | solution.py:163
  99.5 1.3 %select_convert_fusion = bf16[160,2560]{1,0:T(8,128)(2,1)} fusion(bf16[160,2560]{1,0:T(8,128)(2,1)S(1)} %gather_fusion.1, pred[160]{0:T(512)(128)(4,1)S(1)} %get-tuple-element.13, pred[160]{0:T(512)(128)(4,1)S(1)} %fusion.58), kind=kLoop, calls=%fused_computation.14 | loop fusion | flops 819200 | bytes 1638720 | tf_op jit(solution)/shard_map/convert_element_type | solution.py:164
  (38 shorter events, 0.2 us)
Async XLA Ops:
  6.5 69.5 %copy-start = (bf16[5120,256]{1,0:T(8,128)(2,1)S(1)}, bf16[5120,256]{1,0:T(8,128)(2,1)}, u32[]{:S(2)}) copy-start(bf16[5120,256]{1,0:T(8,128)(2,1)} %param.12) | copy-start | bytes 7864324
  6.5 16.0 %all-gather.2.cloned.1.call-start = ((), (), s32[]{:S(2)}) async-start(), calls=%async_computation.2 | async-start | bytes 3440640 | tf_op jit(solution)/shard_map/all_gather | solution.py:58
  11.7 5.3 %copy-start.6 = (s32[8,5]{1,0:T(8,128)S(1)}, s32[8,5]{1,0:T(8,128)}, u32[]{:S(2)}) copy-start(s32[8,5]{1,0:T(8,128)} %param.19) | copy-start | bytes 484
  11.7 5.4 %copy-start.4 = (s32[8,5]{1,0:T(8,128)S(1)}, s32[8,5]{1,0:T(8,128)}, u32[]{:S(2)}) copy-start(s32[8,5]{1,0:T(8,128)} %param.18) | copy-start | bytes 484
  11.7 19.0 %all-to-all-start.1 = ((bf16[256,2,2560]{0,2,1:T(8,128)(2,1)}), bf16[256,2,2560]{0,2,1:T(8,128)(2,1)}, u32[]{:S(2)}, u32[]{:S(2)}) async-start(bf16[256,2,2560]{0,2,1:T(8,128)(2,1)} %bitcast.82), calls=%async_computation.1 | async-start | bytes 5242880 | tf_op jit(solution)/shard_map/all_to_all | solution.py:160
  30.7 38.3 %all-to-all-start = ((bf16[8,16,5120]{2,1,0:T(8,128)(2,1)}), bf16[8,16,5120]{2,1,0:T(8,128)(2,1)}, u32[]{:S(2)}, u32[]{:S(2)}) async-start(bf16[8,16,5120]{2,1,0:T(8,128)(2,1)} %broadcast_select_fusion), calls=%async_computation | async-start | bytes 2621440 | tf_op jit(solution)/shard_map/all_to_all | solution.py:140
  42.0 30.0 %copy-start.5 = (f32[5120]{0:T(1024)S(1)}, f32[5120]{0:T(1024)}, u32[]{:S(2)}) copy-start(f32[5120]{0:T(1024)} %param.11) | copy-start | bytes 61444
  69.1 3.0 %copy-start.1 = (bf16[224,5120]{1,0:T(8,128)(2,1)S(1)}, bf16[224,5120]{1,0:T(8,128)(2,1)}, u32[]{:S(2)}) copy-start(bf16[224,5120]{1,0:T(8,128)(2,1)} %all-gather.2.cloned.1.call-done) | copy-start | bytes 6881284
  74.2 1.8 %copy-start.2 = (bf16[352,5120]{1,0:T(8,128)(2,1)}, bf16[352,5120]{1,0:T(8,128)(2,1)S(1)}, u32[]{:S(2)}) copy-start(bf16[352,5120]{1,0:T(8,128)(2,1)S(1)} %fusion.4) | copy-start | bytes 10813444
  77.9 3.7 %copy-start.7 = (f32[128]{0:T(128)S(1)}, f32[128]{0:T(128)}, u32[]{:S(2)}) copy-start(f32[128]{0:T(128)} %param.16) | copy-start | bytes 1540
  77.9 3.8 %copy-start.8 = (f32[128]{0:T(128)S(1)}, f32[128]{0:T(128)}, u32[]{:S(2)}) copy-start(f32[128]{0:T(128)} %param.17) | copy-start | bytes 1540
  77.9 3.9 %copy-start.9 = (f32[64]{0:T(128)S(1)}, f32[64]{0:T(128)}, u32[]{:S(2)}) copy-start(f32[64]{0:T(128)} %multiply_power_fusion) | copy-start | bytes 772
  81.5 2.1 %copy-start.3 = (pred[224,224]{0,1:T(8,128)(4,1)S(1)}, pred[224,224]{0,1:T(8,128)(4,1)}, u32[]{:S(2)}) copy-start(pred[224,224]{0,1:T(8,128)(4,1)} %compare_and_fusion) | copy-start | bytes 150532
  84.8 3.6 %copy-start.10 = (f32[2,224,224]{1,2,0:T(8,128)S(1)}, f32[2,224,224]{1,2,0:T(8,128)}, u32[]{:S(2)}) copy-start(f32[2,224,224]{1,2,0:T(8,128)} %get-tuple-element.37) | copy-start | bytes 1204228
Sparse Core Ops, SparseCore 0:
  8.9 13.5 all-gather.1
where the time goes:
time: 108 us
  waiting for transfers between devices  30 us (28%)
  local copies, waits for them, and re-layouts  20.9 us (19%)
  matrix products  15.1 us (14%)
  other arithmetic  14.1 us (13%)
  between operations  13.8 us (13%)
  starting transfers between devices  11.6 us (11%)
  blocking collectives  2.24 us (2%)
    all_to_all x1, waiting for transfers between devices, per_device(): lax.all_to_all(outbound, 'dp', split_axis=0, concat_axis=0, tiled=True)  24.8 us
    all_to_all x1, starting transfers between devices, per_device(): lax.all_to_all(outbound, 'dp', split_axis=0, concat_axis=0, tiled=True)  6.46 us
    unnamed x24, local copies, waits for them, and re-layouts  6.35 us
    gather x1, local copies, waits for them, and re-layouts, per_device(): jnp.take(home_full, send_rows, axis=0).reshape(replicas, CAPP, -1)  5.64 us
    all_to_all x1, starting transfers between devices, per_device(): lax.all_to_all(o_weight, 'tensor', split_axis=1, concat_axis=0, tiled=True)  5.14 us
    dot_general x1, matrix products, per_device(): summed = jnp.dot(all_heads, own_columns, preferred_element_type=jnp.float32)  4.54 us
    all_gather x1, waiting for transfers between devices, widen(): return lax.all_gather(half_rows, 'tensor', axis=1, tiled=True)  4.41 us
    all_to_all x1, local copies, waits for them, and re-layouts, per_device(): lax.all_to_all(o_weight, 'tensor', split_axis=1, concat_axis=0, tiled=True)  4.4 us
  transfers between devices with their start and end apart: 3, of which 2 were waited for; matrix products, arithmetic and copies ran while one was open for 19% of the time, Pallas kernels for 0%

commit v1 on v0

--- a/solution.py
+++ b/solution.py
@@ -157,7 +157,12 @@
     head_out = jnp.concatenate([home_out, arrive_out.reshape(replicas * CAPP, -1, HD)], axis=0)
     head_out = head_out.reshape(home_rows + replicas * CAPP, -1).astype(jnp.bfloat16)
     all_heads = lax.all_gather(head_out, "tensor", axis=1, tiled=True)
-    own_columns = lax.all_to_all(o_weight, "tensor", split_axis=1, concat_axis=0, tiled=True)
+    own_columns = jnp.concatenate(
+        lax.all_to_all(
+            jnp.stack(jnp.split(o_weight, lax.axis_size("tensor"), axis=1)), "tensor", 0, 0
+        ),
+        axis=0,
+    )
     summed = jnp.dot(all_heads, own_columns, preferred_element_type=jnp.float32)
     mixed_pool = pool_half.astype(jnp.float32) + summed
     mixed = jnp.where(work_live[:, None], jnp.take(mixed_pool, pool_row, axis=0), 0.0)

time: 108 us -> 113 us (1.046)
  waiting for transfers between devices: 30 us -> 37.7 us
  local copies, waits for them, and re-layouts: 20.9 us -> 15.3 us
  other arithmetic: 14.1 us -> 17.2 us
    all_gather x1, waiting for transfers between devices: 4.41 us -> 10.2 us  [widen(): return lax.all_gather(half_rows, 'tensor', axis=1, tiled=True)]
    unnamed x24 -> x19, local copies, waits for them, and re-layouts: 6.35 us -> 1.82 us
    all_to_all x1 -> x0, local copies, waits for them, and re-layouts: 4.4 us -> none  [per_device(): lax.all_to_all(o_weight, 'tensor', split_axis=1, concat_axis=0, tiled=True)]
    all_to_all x1, waiting for transfers between devices: 24.8 us -> 26.8 us  [per_device(): lax.all_to_all(outbound, 'dp', split_axis=0, concat_axis=0, tiled=True)]
    another operation x0 -> x1, local copies, waits for them, and re-layouts: none -> 1.88 us  [per_device(): jnp.stack(jnp.split(o_weight, lax.axis_size('tensor'), axis=1))]
    another operation x1 -> x2, other arithmetic: 0.19 us -> 1.97 us  [the longest x1 1.78 us: per_device(): jnp.stack(jnp.split(o_weight, lax.axis_size('tensor'), axis=1))]
  transfers between devices with their start and end apart: 3 -> 3, of which waited for: 2 -> 2; matrix products, arithmetic and copies ran while one was open for 19% -> 25% of each run, Pallas kernels for 0% -> 0%
where the time goes in v1:
time: 113 us; the launch traced here: 112 us
  waiting for transfers between devices  37.7 us (33%)
  other arithmetic  17.2 us (15%)
  local copies, waits for them, and re-layouts  15.3 us (14%)
  matrix products  15.1 us (13%)
  between operations  13.8 us (12%)
  starting transfers between devices  10.8 us (10%)
  blocking collectives  2.35 us (2%)
    all_to_all x1, waiting for transfers between devices, per_device(): lax.all_to_all(outbound, 'dp', split_axis=0, concat_axis=0, tiled=True)  26.8 us
    all_gather x1, waiting for transfers between devices, widen(): return lax.all_gather(half_rows, 'tensor', axis=1, tiled=True)  10.2 us
    all_to_all x1, starting transfers between devices, per_device(): lax.all_to_all(outbound, 'dp', split_axis=0, concat_axis=0, tiled=True)  5.77 us
    gather x1, local copies, waits for them, and re-layouts, per_device(): jnp.take(home_full, send_rows, axis=0).reshape(replicas, CAPP, -1)  5.63 us
    all_to_all x1, starting transfers between devices, per_device(): lax.all_to_all(jnp.stack(jnp.split(o_weight, lax.axis_size('tensor'), axi...  5.01 us
    dot_general x1, matrix products, per_device(): summed = jnp.dot(all_heads, own_columns, preferred_element_type=jnp.float32)  4.54 us
    gather x1, local copies, waits for them, and re-layouts, per_device(): jnp.take(mixed_pool, pool_row, axis=0)  3.63 us
    dot_general x1, matrix products, project(): key_rows = jnp.dot(normed, k_weight, preferred_element_type=jnp.float32)  3.6 us
  transfers between devices with their start and end apart: 3, of which 2 were waited for; matrix products, arithmetic and copies ran while one was open for 25% of the time, Pallas kernels for 0%

profile of v1, /device:TPU:0, one launch (start us, length us, event | category | flops | bytes accessed | tf_op | source)
XLA Modules:
  0.0 112.1 jit_solution(11339923883213322993)
XLA Ops:
  6.5 0.0 copy-start
  6.5 0.0 all-gather.2.cloned.1.call-start
  6.5 0.7 all-gather.2.cloned.1.call-update
  7.3 0.1 reshape.679
  7.4 0.8 reshape.678
  8.1 0.1 reshape.680
  8.2 0.8 broadcast_in_dim.197
  9.0 0.8 reduce_window_sum.11
  9.8 0.7 sub.80
  10.5 0.1 reshape.681
  10.6 0.2 select_reduce_fusion.6
  10.9 0.2 select_reduce_fusion
  11.1 0.1 reshape.682
  11.2 0.4 fusion.20
  11.5 0.1 concatenate.30
  11.6 0.1 select_reduce_fusion.2
  11.7 0.1 add_convert_fusion.2
  11.8 0.1 select_reduce_fusion.3
  12.0 0.2 and_reduce_fusion
  12.2 0.1 fusion.59
  12.3 10.2 %all-gather.2.cloned.1.call-done = bf16[224,5120]{1,0:T(8,128)(2,1)} async-done(((bf16[224,2560]{1,0:T(8,128)(2,1)}), bf16[224,5120]{1,0:T(8,128)(2,1)}) %all-gather.2.cloned.1.call-update) | async-done | bytes 2293776 | tf_op jit(solution)/shard_map/all_gather | solution.py:58
  22.5 5.6 %gather_fusion = bf16[128,5120]{1,0:T(8,128)(2,1)} fusion(bf16[224,5120]{1,0:T(8,128)(2,1)} %all-gather.2.cloned.1.call-done, s32[1024]{0:T(1024)S(1)} %pad_clamp_fusion.1), kind=kCustom, calls=%fused_computation | custom fusion | bytes 2621952 | tf_op jit(solution)/shard_map/jit(_take)/gather | solution.py:139
  28.1 2.6 %broadcast_select_fusion = bf16[8,16,5120]{2,1,0:T(8,128)(2,1)} fusion(bf16[8,16,5120]{2,1,0:T(8,128)(2,1)} %bitcast.84, pred[8,16]{1,0:T(8,128)(4,1)S(1)} %compare_and_fusion.4), kind=kLoop, calls=%fused_computation.18 | loop fusion | flops 655360 | bytes 2621568 | tf_op jit(solution)/shard_map/jit(_take)/select_n | solution.py:139
  30.7 5.8 %all-to-all-start = ((bf16[8,16,5120]{2,1,0:T(8,128)(2,1)}), bf16[8,16,5120]{2,1,0:T(8,128)(2,1)}, u32[]{:S(2)}, u32[]{:S(2)}) async-start(bf16[8,16,5120]{2,1,0:T(8,128)(2,1)} %broadcast_select_fusion), calls=%async_computation | async-start | bytes 2621440 | tf_op jit(solution)/shard_map/all_to_all | solution.py:140
  36.5 0.5 multiply_power_fusion
  37.0 0.1 fusion.58
  37.1 0.1 compare_and_fusion.1
  37.2 0.8 compare_and_fusion
  38.0 1.9 %slice_bitcast_fusion.1 = (bf16[1,256,2560]{2,1,0:T(8,128)(2,1)S(1)}, bf16[1,256,2560]{2,1,0:T(8,128)(2,1)S(1)}) fusion(bf16[256,5120]{1,0:T(8,128)(2,1)} %param.15), kind=kLoop, calls=%fused_computation.17 | loop fusion | bytes 5242880 | tf_op jit(solution)/shard_map/stack | solution.py:162
  39.9 1.8 %pad_maximum_fusion.1 = bf16[2,256,2560]{2,1,0:T(8,128)(2,1)} fusion(bf16[1,256,2560]{2,1,0:T(8,128)(2,1)S(1)} %get-tuple-element.16, bf16[1,256,2560]{2,1,0:T(8,128)(2,1)S(1)} %get-tuple-element.15), kind=kLoop, calls=%fused_computation.13 | loop fusion | flops 1310720 | bytes 5242880 | tf_op jit(solution)/shard_map/stack | solution.py:162
  41.7 26.8 %all-to-all-done = bf16[8,16,5120]{2,1,0:T(8,128)(2,1)} async-done(((bf16[8,16,5120]{2,1,0:T(8,128)(2,1)}), bf16[8,16,5120]{2,1,0:T(8,128)(2,1)}, u32[]{:S(2)}, u32[]{:S(2)}) %all-to-all-start) | async-done | bytes 1310752 | tf_op jit(solution)/shard_map/all_to_all | solution.py:140
  68.4 5.0 %all-to-all-start.1 = ((bf16[2,256,2560]{2,1,0:T(8,128)(2,1)}), bf16[2,256,2560]{2,1,0:T(8,128)(2,1)}, u32[]{:S(2)}, u32[]{:S(2)}) async-start(bf16[2,256,2560]{2,1,0:T(8,128)(2,1)} %pad_maximum_fusion.1), calls=%async_computation.1 | async-start | bytes 5242880 | tf_op jit(solution)/shard_map/all_to_all | solution.py:161
  73.4 0.0 copy-start.1
  73.5 0.0 copy-start.4
  73.5 3.0 %fusion.2 = f32[352]{0:T(512)S(1)} fusion(bf16[128,5120]{1,0:T(8,128)(2,1)} %bitcast.2, bf16[224,5120]{1,0:T(8,128)(2,1)} %all-gather.2.cloned.1.call-done), kind=kLoop, calls=%fused_computation.6 | loop fusion | flops 10813088 | bytes 3605888 | tf_op jit(solution)/shard_map/reduce_sum | solution.py:16
  76.5 0.0 copy-done.1
  76.5 2.1 %fusion.4 = bf16[352,5120]{1,0:T(8,128)(2,1)S(1)} fusion(f32[5120]{0:T(1024)S(1)} %copy-done.4, f32[352]{0:T(512)S(1)} %add_rsqrt_fusion.2, bf16[128,5120]{1,0:T(8,128)(2,1)} %bitcast.2, bf16[224,5120]{1,0:T(8,128)(2,1)S(1)} %copy-done.1), kind=kLoop, calls=%fused_computation.8 | loop fusion | flops 12615680 | bytes 7230848 | tf_op jit(solution)/shard_map/convert_element_type | solution.py:63
  78.6 1.8 %copy-done.2 = bf16[352,5120]{1,0:T(8,128)(2,1)} copy-done((bf16[352,5120]{1,0:T(8,128)(2,1)}, bf16[352,5120]{1,0:T(8,128)(2,1)S(1)}, u32[]{:S(2)}) %copy-start.2) | copy-done | bytes 3604504
  80.4 0.0 copy-done
  80.4 1.1 fusion.68
  81.5 0.2 reshape.684
  81.7 0.4 multiply_reduce_fusion
  82.1 0.1 copy.35
  82.2 0.0 copy-start.5
  82.3 0.0 copy-start.6
  82.3 3.6 %multiply_reduce_fusion.1 = (f32[352]{0:T(512)S(1)}, f32[352,128]{1,0:T(8,128)S(1)}) fusion(bf16[352,5120]{1,0:T(8,128)(2,1)} %copy-done.2, bf16[5120,128]{1,0:T(8,128)(2,1)} %param.13), kind=kOutput, calls=%fused_computation.49 | convolution fusion | flops 461463200 | bytes 5096832 | tf_op jit(solution)/shard_map/dot_general | solution.py:71
  85.9 0.2 fusion.16
  86.1 0.1 multiply_multiply_fusion
  86.2 0.8 multiply_cosine_fusion
  87.0 0.2 subtract_convert_fusion
  87.2 0.1 pad_maximum_fusion.3
  87.3 0.1 pad_maximum_fusion.4
  87.4 0.3 fusion.13
  87.6 0.3 fusion.60
  88.0 1.2 %fusion.63 = (f32[2,224]{1,0:T(2,128)S(1)}, f32[2,224,224]{1,2,0:T(8,128)}) fusion(pred[224,224]{0,1:T(8,128)(4,1)S(1)} %copy-done.3, bf16[352,2,64]{2,0,1:T(8,128)(2,1)S(1)} %get-tuple-element.17, bf16[352,2,64]{2,0,1:T(8,128)(2,1)S(1)} %get-tuple-element.18, bf16[352,64]{1,0:T(8,128)(2,1)S(1)} %get-tuple-element.24, ...), kind=kOutput, calls=%fused_computation.133 | convolution fusion | flops 26435808 | bytes 723712 | tf_op jit(solution)/shard_map/sub | solution.py:84
  89.1 3.5 %convolution_convert_fusion.1 = bf16[352,128]{1,0:T(8,128)(2,1)S(1)} fusion(bf16[352,5120]{1,0:T(8,128)(2,1)} %copy-done.2, bf16[5120,128]{1,0:T(8,128)(2,1)} %param.14), kind=kOutput, calls=%fused_computation.26 | convolution fusion | flops 461418496 | bytes 5005312 | tf_op jit(solution)/shard_map/dot_general | solution.py:73
  92.7 0.3 fusion.14
  93.0 0.2 fusion.15
  93.3 0.1 copy.41
  93.4 2.3 %all_gather.7 = bf16[352,512]{1,0:T(8,128)(2,1)S(1)} all-gather(bf16[352,256]{1,0:T(8,128)(2,1)S(1)} %pad_maximum_fusion.2), channel_id=1, replica_groups=mesh['groups'=2,'dp'=8,'tensor'=2] {'tensor'}, dimensions={1}, use_global_device_ids=true | all-gather | bytes 540672 | tf_op jit(solution)/shard_map/all_gather | solution.py:159
  95.7 0.0 all-to-all-done.1
  95.7 4.5 %convolution_add_fusion = bf16[352,2560]{1,0:T(8,128)(2,1)} fusion(bf16[352,512]{1,0:T(8,128)(2,1)S(1)} %all_gather.7, bf16[512,2560]{1,0:T(8,128)(2,1)} %bitcast.18, s32[]{:T(128)S(6)} %select_n.145, bf16[224,5120]{1,0:T(8,128)(2,1)} %all-gather.2.cloned.1.call-done, bf16[128,5120]{1,0:T(8,128)(2,1)} %bitcast.2), kind=kOutput, calls=%fused_computation.9 | convolution fusion | flops 928153600 | bytes 8388612 | tf_op jit(solution)/shard_map/dot_general | solution.py:166
  100.3 3.6 %gather_fusion.1 = bf16[160,2560]{1,0:T(8,128)(2,1)S(1)} fusion(bf16[352,2560]{1,0:T(8,128)(2,1)} %convolution_add_fusion, s32[1024]{0:T(1024)S(1)} %pad_clamp_fusion), kind=kCustom, calls=%fused_computation.1 | custom fusion | bytes 1639040 | tf_op jit(solution)/shard_map/jit(_take)/gather | solution.py:168
  103.9 1.3 %select_convert_fusion = bf16[160,2560]{1,0:T(8,128)(2,1)} fusion(bf16[160,2560]{1,0:T(8,128)(2,1)S(1)} %gather_fusion.1, pred[160]{0:T(512)(128)(4,1)S(1)} %get-tuple-element.13, pred[160]{0:T(512)(128)(4,1)S(1)} %fusion.58), kind=kLoop, calls=%fused_computation.15 | loop fusion | flops 819200 | bytes 1638720 | tf_op jit(solution)/shard_map/convert_element_type | solution.py:169
  (34 shorter events, 0.2 us)
Async XLA Ops:
  6.5 73.8 %copy-start = (bf16[5120,256]{1,0:T(8,128)(2,1)S(1)}, bf16[5120,256]{1,0:T(8,128)(2,1)}, u32[]{:S(2)}) copy-start(bf16[5120,256]{1,0:T(8,128)(2,1)} %param.12) | copy-start | bytes 7864324
  6.5 16.0 %all-gather.2.cloned.1.call-start = ((), (), s32[]{:S(2)}) async-start(), calls=%async_computation.2 | async-start | bytes 3440640 | tf_op jit(solution)/shard_map/all_gather | solution.py:58
  30.7 37.7 %all-to-all-start = ((bf16[8,16,5120]{2,1,0:T(8,128)(2,1)}), bf16[8,16,5120]{2,1,0:T(8,128)(2,1)}, u32[]{:S(2)}, u32[]{:S(2)}) async-start(bf16[8,16,5120]{2,1,0:T(8,128)(2,1)} %broadcast_select_fusion), calls=%async_computation | async-start | bytes 2621440 | tf_op jit(solution)/shard_map/all_to_all | solution.py:140
  68.4 27.3 %all-to-all-start.1 = ((bf16[2,256,2560]{2,1,0:T(8,128)(2,1)}), bf16[2,256,2560]{2,1,0:T(8,128)(2,1)}, u32[]{:S(2)}, u32[]{:S(2)}) async-start(bf16[2,256,2560]{2,1,0:T(8,128)(2,1)} %pad_maximum_fusion.1), calls=%async_computation.1 | async-start | bytes 5242880 | tf_op jit(solution)/shard_map/all_to_all | solution.py:161
  73.4 3.0 %copy-start.1 = (bf16[224,5120]{1,0:T(8,128)(2,1)S(1)}, bf16[224,5120]{1,0:T(8,128)(2,1)}, u32[]{:S(2)}) copy-start(bf16[224,5120]{1,0:T(8,128)(2,1)} %all-gather.2.cloned.1.call-done) | copy-start | bytes 6881284
  73.5 3.0 %copy-start.4 = (f32[5120]{0:T(1024)S(1)}, f32[5120]{0:T(1024)}, u32[]{:S(2)}) copy-start(f32[5120]{0:T(1024)} %param.11) | copy-start | bytes 61444
  78.6 1.8 %copy-start.2 = (bf16[352,5120]{1,0:T(8,128)(2,1)}, bf16[352,5120]{1,0:T(8,128)(2,1)S(1)}, u32[]{:S(2)}) copy-start(bf16[352,5120]{1,0:T(8,128)(2,1)S(1)} %fusion.4) | copy-start | bytes 10813444
  82.2 3.7 %copy-start.5 = (f32[128]{0:T(128)S(1)}, f32[128]{0:T(128)}, u32[]{:S(2)}) copy-start(f32[128]{0:T(128)} %param.16) | copy-start | bytes 1540
  82.3 3.8 %copy-start.6 = (f32[128]{0:T(128)S(1)}, f32[128]{0:T(128)}, u32[]{:S(2)}) copy-start(f32[128]{0:T(128)} %param.17) | copy-start | bytes 1540
  82.3 3.9 %copy-start.7 = (f32[64]{0:T(128)S(1)}, f32[64]{0:T(128)}, u32[]{:S(2)}) copy-start(f32[64]{0:T(128)} %multiply_power_fusion) | copy-start | bytes 772
  85.9 2.1 %copy-start.3 = (pred[224,224]{0,1:T(8,128)(4,1)S(1)}, pred[224,224]{0,1:T(8,128)(4,1)}, u32[]{:S(2)}) copy-start(pred[224,224]{0,1:T(8,128)(4,1)} %compare_and_fusion) | copy-start | bytes 150532
  89.1 3.6 %copy-start.8 = (f32[2,224,224]{1,2,0:T(8,128)S(1)}, f32[2,224,224]{1,2,0:T(8,128)}, u32[]{:S(2)}) copy-start(f32[2,224,224]{1,2,0:T(8,128)} %get-tuple-element.39) | copy-start | bytes 1204228
Sparse Core Ops, SparseCore 0:
  8.9 13.5 all-gather.1
